TPU v7x, 512 devices: a whole 4x4x16 slice. The times are simulated.
512 devices in a mesh: pool: 64 (over y, z), ctx: 8 (over x, core).
Axes of the slice: x: 4, y: 4, z: 16, core: 2. Of those that a mesh axis runs over, the one named last changes fastest.
Arguments:
- fresh_q: bfloat16 [4096, 8192], P('pool', 'ctx'), may hold values from -180 to 180
- fresh_kv: bfloat16 [4096, 2048], P('pool', 'ctx'), may hold values from -6 to 6
- pool_kv: bfloat16 [256, 512, 2048], P(None, 'pool', 'ctx'), may hold values from -6 to 6
- passage_lists: int32 [4, 32], replicated, may hold values from 0 to 255
- slot_map: int32 [256], replicated, may hold values from 0 to 255, each once
- rec_pos: int32 [64, 64], P('pool'), may hold values from 0 to 1023, as said below
Outputs:
- attn_out: bfloat16 [4096, 8192], P('pool', 'ctx')
- deviation: float32 [4096], P('pool')
Inputs may be any that keep to these rules, and one draw needn't show every extreme that they name: `rec_pos`: the 64 offsets of one tile are distinct. `slot_map`: each passage has a row of its own in the store.
All inputs are finite; a program needn't handle non-finite values.
Results may differ from a plain program's by a relative error of at most 0.017.
Values may be sent and summed in bfloat16 or wider, within the bound.
A program may use at most 64 MiB of HBM per device.

v0:
```python
import math

import jax
import jax.numpy as jnp
import numpy as np
from jax import lax
from jax.experimental import pallas as pl
from jax.experimental.pallas import tpu as pltpu
from jax.sharding import PartitionSpec as P

HEADS = 64
KVH = 8
HD = 128
PASSAGE = 512
BLOCK_PASSAGES = 2
SEQ_BLOCKS = 16
ROWS = 64
REQS = 4
CTX = 8
SPAN = BLOCK_PASSAGES * PASSAGE
BASE = 500000.0

MESH = pl.DeviceIdType.MESH
F32 = jnp.float32
BF16 = jnp.bfloat16
LOG2_SCALE = math.log2(math.e) / math.sqrt(HD)
NEG = -1e30
FAR = 1 << 30
STEPS = 4


def frequency_table():
    exponent = np.arange(HD // 2, dtype=np.float32) * np.float32(-2.0 * math.log(BASE) / HD)
    return np.exp(exponent.astype(np.float64)).astype(np.float32)


def passage_tables():
    offsets = np.arange(SEQ_BLOCKS * BLOCK_PASSAGES).astype(np.float32) * np.float32(PASSAGE)
    angles = (offsets[:, None] * frequency_table()[None, :]).astype(np.float64)
    cosine, sine = np.cos(angles), np.sin(angles)
    return (
        np.concatenate([cosine, cosine], axis=1).astype(np.float32),
        np.concatenate([-sine, sine], axis=1).astype(np.float32),
    )


def turned(vectors, cosine, signed_sine):
    half = HD // 2
    swapped = jnp.concatenate([vectors[:, half:], vectors[:, :half]], axis=1)
    return vectors * cosine + swapped * signed_sine


def iota(shape, axis):
    return lax.broadcasted_iota(jnp.int32, shape, axis)


def kernel(
    lists, slots, rec_ref, q_ref, fkv_ref, pool_ref, freq_ref, cos_ref, sin_ref,
    out_ref, dev_ref,
    pack, kvb, vt, kpos, fkv, fkv_in, vtf, fpos, recs, qown, qbuf, kf_own, kfbuf,
    part, pstat, osend, ssend, orecv, srecv, dsend, drecv, xbuf,
    kv_ss, kv_rs, rec_ss, rec_rs, f_ss, f_rs, q_ss, q_rs, kf_ss, kf_rs,
    o_ss, o_rs, s_ss, s_rs, d_ss, d_rs, x_ss, x_rs,
):
    where = lax.axis_index("pool")
    me_ctx = lax.axis_index("ctx")
    y = where // SEQ_BLOCKS
    z = where % SEQ_BLOCKS

    def node(row, column):
        return {"pool": (row % REQS) * SEQ_BLOCKS + (column + SEQ_BLOCKS) % SEQ_BLOCKS}

    def remote(src, dst, send, recv, target):
        return pltpu.make_async_remote_copy(
            src_ref=src, dst_ref=dst, send_sem=send, recv_sem=recv,
            device_id=target, device_id_type=MESH,
        )

    barrier = pltpu.get_barrier_semaphore()

    def greet(target):
        pl.semaphore_signal(barrier, inc=1, device_id=target, device_id_type=MESH)

    for k in range(1, SEQ_BLOCKS):
        greet(node(y, z + k))
    for row in range(1, REQS):
        for column in (-1, 0, 1):
            greet(node(y + row, z + column))
    for k in range(1, CTX):
        greet({"ctx": (me_ctx + k) % CTX})

    rec_row = rec_ref[...]
    rec_pair = jnp.concatenate([rec_row, rec_row], axis=1)
    recs[z] = rec_pair
    diagonal = iota((HD, HD), 0) == iota((HD, HD), 1)

    def as_column(row):
        wide = jnp.broadcast_to(row.astype(F32), (HD, HD))
        return jnp.sum(jnp.where(diagonal, wide, 0.0), axis=1, keepdims=True)

    rows_at = as_column(rec_pair)[:ROWS] + (z * SPAN).astype(F32)
    angles = rows_at * freq_ref[...]
    cosine = jnp.cos(angles)
    sine = jnp.where(iota((ROWS, HD), 1) < HD // 2, -jnp.sin(angles), jnp.sin(angles))
    for pair in range(4):
        both = [
            turned(q_ref[:, (2 * pair + i) * HD : (2 * pair + i + 1) * HD].astype(F32), cosine, sine)
            for i in range(2)
        ]
        stacked = jnp.concatenate(both, axis=0)
        qown[pair // 2, :, (pair % 2) * HD : (pair % 2 + 1) * HD] = stacked.T.astype(BF16)
    fresh_key = turned(fkv_ref[:, :HD].astype(F32), cosine, sine).astype(BF16)
    kf_own[...] = fresh_key
    fkv[:, :HD] = fresh_key
    fkv[:, HD:] = fkv_ref[:, HD:]

    @pl.loop(0, REQS)
    def _(request):
        @pl.loop(0, SEQ_BLOCKS)
        def _(block):
            keys, values = [], []
            for p in range(BLOCK_PASSAGES):
                passage = block * BLOCK_PASSAGES + p
                stored = pool_ref[slots[lists[request, passage]]]
                keys.append(
                    turned(
                        stored[:, :HD].astype(F32),
                        cos_ref[pl.ds(passage, 1), :],
                        sin_ref[pl.ds(passage, 1), :],
                    )
                )
                values.append(stored[:, HD:].astype(F32))
            pack[request, block, :, :HD] = jnp.concatenate(keys, axis=0).astype(BF16)
            pack[request, block, :, HD:] = jnp.concatenate(values, axis=0).astype(BF16)

    pl.semaphore_wait(barrier, SEQ_BLOCKS - 1 + 3 * (REQS - 1) + CTX - 1)

    def q_copy(d, s, c):
        src = qown.at[c] if s == 0 else qbuf.at[d, s - 1, c]
        return remote(
            src, qbuf.at[d, s, c], q_ss.at[d, s, c], q_rs.at[d, s, c], node(y, z + (2 - 4 * d))
        )

    def kf_copy(d, s):
        src = kf_own if s == 0 else kfbuf.at[d, s - 1]
        return remote(src, kfbuf.at[d, s], kf_ss.at[d, s], kf_rs.at[d, s], node(y, z + (2 - 4 * d)))

    def side(row_a, row_b):
        return 2 * (((row_a + row_b) % 4) // 2) - 1

    def kv_copy(i, step):
        row = (y + step) % REQS
        shift = side(y, row) if i else 0
        slot = i * REQS + y
        return remote(
            pack.at[row], kvb.at[:, slot], kv_ss.at[i, step], kv_rs.at[slot], node(row, z + shift)
        )

    def rec_copy(k):
        return remote(recs.at[z], recs.at[z], rec_ss.at[k], rec_rs.at[z], node(y, z + k))

    def fresh_copy():
        return remote(fkv, fkv_in, f_ss.at[0], f_rs.at[0], node(y, z + 1))

    def out_copies(d, s, c):
        target = node(y, z - (2 - 4 * d))
        return (
            remote(ssend.at[d, s, c], srecv.at[d, s, c], s_ss.at[d, s, c], s_rs.at[d, s, c], target),
            remote(osend.at[d, s, c], orecv.at[d, s, c], o_ss.at[d, s, c], o_rs.at[d, s, c], target),
        )

    def dev_copy(k):
        return remote(dsend.at[k], drecv.at[k], d_ss.at[k], d_rs.at[k], node(y, z - 2 * k))

    def ctx_copy(k):
        return remote(
            xbuf.at[me_ctx], xbuf.at[me_ctx], x_ss.at[k], x_rs.at[me_ctx],
            {"ctx": (me_ctx + k) % CTX},
        )

    own_kv = pltpu.make_async_copy(pack.at[y], kvb.at[:, y], kv_rs.at[y])

    for k in range(1, SEQ_BLOCKS):
        rec_copy(k).start()
    for c in range(2):
        for d in range(2):
            q_copy(d, 0, c).start()
    own_kv.start()
    for step in range(1, REQS):
        kv_copy(0, step).start()
    for step in range(REQS):
        kv_copy(1, step).start()
    for d in range(2):
        kf_copy(d, 0).start()
    fresh_copy().start()

    def rec_wait(k):
        other = (z + k) % SEQ_BLOCKS
        remote(recs.at[z], recs.at[other], rec_ss.at[k], rec_rs.at[other], node(y, z + k)).wait_recv()

    for k in range(1, SEQ_BLOCKS):
        rec_wait(k)
    key = iota((HD, HD), 0)
    key_row = (key >> 4) & 3
    key_side = ((y + key_row) & 3) & 2
    key_column = (z - (key >> 6) * (key_side - 1) + SEQ_BLOCKS) & (SEQ_BLOCKS - 1)
    offset = ((key >> 3) & 1) * PASSAGE + key_row * 128 + key_column * 8 + (key & 7)

    @pl.loop(0, SEQ_BLOCKS)
    def _(block):
        same = jnp.where(offset == recs[block], 1.0, 0.0)
        replaced = jnp.max(same, axis=1, keepdims=True) > 0.0
        kpos[block] = jnp.where(replaced, FAR, offset + block * SPAN)

    before = (z + SEQ_BLOCKS - 1) % SEQ_BLOCKS
    fresh_row = jnp.where(
        iota((1, HD), 1) < ROWS, recs[z] + z * SPAN, recs[before] + before * SPAN
    )
    fpos[...] = jnp.broadcast_to(as_column(fresh_row), (HD, HD)).astype(jnp.int32)

    def forward(s, everything):
        for c in range(2):
            for d in range(2):
                q_copy(d, s, c).wait_recv()
                if everything or c == d:
                    q_copy(d, s + 1, c).start()
        for d in range(2):
            kf_copy(d, s).wait_recv()
            if everything or d == 0:
                kf_copy(d, s + 1).start()

    def advance(carried, query, seen, keys, values_t):
        top, total, acc = carried
        scores = jnp.dot(keys, query, preferred_element_type=F32)
        scores = jnp.where(jnp.concatenate([seen, seen], axis=1), scores, NEG)
        new_top = jnp.maximum(top, jnp.max(scores, axis=0, keepdims=True))
        weights = jnp.exp2((scores - new_top) * LOG2_SCALE)
        factor = jnp.exp2((top - new_top) * LOG2_SCALE)
        total = total * factor + jnp.sum(weights, axis=0, keepdims=True)
        acc = acc * factor + jnp.dot(values_t, weights.astype(BF16), preferred_element_type=F32)
        return new_top, total, acc

    def attend(tile, query, slot):
        at = recs[tile] + tile * SPAN
        fresh_keys = jnp.concatenate([fkv[:, :HD], fkv_in[:, :HD]], axis=0)
        start = (
            jnp.full((1, 2 * HD), NEG, F32),
            jnp.zeros((1, 2 * HD), F32),
            jnp.zeros((HD, 2 * HD), F32),
        )
        carried = advance(start, query, fpos[...] <= at, fresh_keys, vtf[...])

        def group(g, carried):
            keys = kvb[pl.ds(2 * g, 2), :, :, :HD].reshape(2 * HD, HD)
            seen = kpos[pl.ds(2 * g, 2)].reshape(2 * HD, HD) <= at
            return advance(carried, query, seen, keys, vt[g])

        top, total, acc = lax.fori_loop(0, tile // 2 + 1, group, carried)
        part[slot] = acc
        pstat[slot, 0:1, :] = top
        pstat[slot, 1:2, :] = total

    def gap_of(tile, keys, k):
        same = jnp.where(offset == recs[tile], 1.0, 0.0)[:, :ROWS].astype(BF16)
        cached = kvb[pl.ds(tile, 1), :, :, :HD].reshape(HD, HD)
        over = (((0,), (0,)), ((), ()))
        found = lax.dot_general(same, cached, over, preferred_element_type=F32)
        hit = lax.dot_general(same, jnp.ones((HD, HD), BF16), over, preferred_element_type=F32)
        gap = (found - keys.astype(F32)) * hit
        squares = (gap * gap).T
        dsend[k, :, :ROWS] = jnp.sum(squares, axis=0, keepdims=True)

    def tile_of(d, s):
        return (z - (2 - 4 * d) * (s + 1) + SEQ_BLOCKS) % SEQ_BLOCKS

    def jobs(s, first, count):
        @pl.loop(first, first + count)
        def _(i):
            d, c = i % 2, i // 2
            attend(tile_of(d, s), qbuf[d, s, c], (s * 2 + d) * 2 + c)

    def far_jobs():
        @pl.loop(0, 2)
        def _(d):
            s = STEPS - 1
            attend(tile_of(d, s), qbuf[d, s, d], (s * 2 + d) * 2 + d)

    def gaps(s):
        for d in range(2):
            if s == STEPS - 1 and d:
                continue
            k = s + 1 if d == 0 else SEQ_BLOCKS // 2 - s - 1
            gap_of(tile_of(d, s), kfbuf[d, s], k)
            dev_copy(k).start()

    dsend[...] = jnp.zeros_like(dsend)
    forward(0, True)

    for slot in range(2 * REQS):
        pltpu.make_async_copy(pack.at[0], kvb.at[:, slot], kv_rs.at[slot]).wait()
    fresh_copy().wait_recv()

    @pl.loop(0, SEQ_BLOCKS // 2)
    def _(g):
        for i in range(2):
            values = kvb[pl.ds(2 * g + i, 1), :, :, HD:].reshape(HD, HD)
            vt[g, :, i * HD : (i + 1) * HD] = values.astype(F32).T.astype(BF16)

    fresh_values = jnp.concatenate([fkv[:, HD:], fkv_in[:, HD:]], axis=0)
    vtf[...] = fresh_values.astype(F32).T.astype(BF16)

    @pl.loop(0, 2)
    def _(c):
        attend(z, qown[c], 16 + c)

    forward(1, True)
    jobs(0, 0, 4)
    gap_of(z, kf_own[...], 0)
    gaps(0)
    forward(2, False)
    jobs(1, 0, 4)
    gaps(1)
    jobs(2, 0, 4)

    def merged(d, s, c, slot):
        top, total, acc = pstat[slot, 0:1, :], pstat[slot, 1:2, :], part[slot]
        stats, far = out_copies(d, s, c)
        stats.wait_recv()
        other = srecv[d, s, c]
        other_top = jnp.concatenate([other[0:1, :], other[1:2, :]], axis=1)
        other_total = jnp.concatenate([other[2:3, :], other[3:4, :]], axis=1)
        new_top = jnp.maximum(top, other_top)
        mine = jnp.exp2((top - new_top) * LOG2_SCALE)
        theirs = jnp.exp2((other_top - new_top) * LOG2_SCALE)
        total = total * mine + other_total * theirs
        far.wait_recv()
        acc = acc * mine + orecv[d, s, c].astype(F32) * theirs
        return new_top, total, acc

    def hand_on(d, s, c):
        slot = (s * 2 + d) * 2 + c
        if s == STEPS - 1 or (s == STEPS - 2 and c != d):
            top, total, acc = pstat[slot, 0:1, :], pstat[slot, 1:2, :], part[slot]
        else:
            top, total, acc = merged(d, s + 1, c, slot)
        ssend[d, s, c, 0:1, :] = top[:, :HD]
        ssend[d, s, c, 1:2, :] = top[:, HD:]
        ssend[d, s, c, 2:3, :] = total[:, :HD]
        ssend[d, s, c, 3:4, :] = total[:, HD:]
        osend[d, s, c] = acc.astype(BF16)
        for copy in out_copies(d, s, c):
            copy.start()

    ssend[...] = jnp.zeros_like(ssend)
    for d in range(2):
        hand_on(d, 2, 1 - d)
    for d in range(2):
        q_copy(d, 3, d).wait_recv()
    far_jobs()
    for d in range(2):
        hand_on(d, 3, d)
    kf_copy(0, 3).wait_recv()
    gaps(2)
    gaps(3)
    for d in range(2):
        hand_on(d, 1, 1 - d)
    for k in range(1, 8):
        dev_copy(k).wait_recv()
    shared = dsend[0]
    for k in range(1, 8):
        shared = shared + drecv[k]
    xbuf[me_ctx] = shared
    for k in range(1, CTX):
        ctx_copy(k).start()
    for d in range(2):
        hand_on(d, 2, d)
    for d in range(2):
        hand_on(d, 0, 1 - d)
    for d in range(2):
        hand_on(d, 1, d)
    for d in range(2):
        hand_on(d, 0, d)

    for k in range(1, CTX):
        other = (me_ctx + k) % CTX
        remote(
            xbuf.at[me_ctx], xbuf.at[other], x_ss.at[k], x_rs.at[other], {"ctx": other}
        ).wait_recv()
    gathered = xbuf[0]
    for k in range(1, CTX):
        gathered = gathered + xbuf[k]
    dev_ref[...] = gathered[:, :ROWS] / (KVH * HD)

    for c in range(2):
        slot = 16 + c
        for d in ((0, 1) if c else (1, 0)):
            top, total, acc = merged(d, 0, c, slot)
            pstat[slot, 0:1, :] = top
            pstat[slot, 1:2, :] = total
            part[slot] = acc
        done = part[slot] / pstat[slot, 1:2, :]
        for pair in range(2):
            upright = done[:, pair * HD : (pair + 1) * HD].T.astype(BF16)
            for i in range(2):
                head = c * 4 + pair * 2 + i
                out_ref[:, head * HD : (head + 1) * HD] = upright[i * ROWS : (i + 1) * ROWS]

    for k in range(1, SEQ_BLOCKS):
        rec_copy(k).wait_send()
    for step in range(REQS):
        if step:
            kv_copy(0, step).wait_send()
        kv_copy(1, step).wait_send()
    fresh_copy().wait_send()
    for d in range(2):
        for s in range(STEPS):
            for c in range(2):
                if s < STEPS - 1 or c == d:
                    q_copy(d, s, c).wait_send()
                    for copy in out_copies(d, s, c):
                        copy.wait_send()
            if s < STEPS - 1 or d == 0:
                kf_copy(d, s).wait_send()
    for k in range(1, 8):
        dev_copy(k).wait_send()
    for k in range(1, CTX):
        ctx_copy(k).wait_send()


def on_device(fresh_q, fresh_kv, pool_kv, passage_lists, slot_map, rec_pos):
    freq = frequency_table()
    freq = jnp.asarray(np.concatenate([freq, freq])[None, :])
    cosine, sine = (jnp.asarray(table) for table in passage_tables())
    vmem = pl.BlockSpec(memory_space=pltpu.VMEM)
    smem = pl.BlockSpec(memory_space=pltpu.SMEM)
    dma = pltpu.SemaphoreType.DMA
    output, deviation = pl.pallas_call(
        kernel,
        out_shape=(
            jax.ShapeDtypeStruct((ROWS, HEADS // CTX * HD), BF16),
            jax.ShapeDtypeStruct((1, ROWS), F32),
        ),
        in_specs=[smem, smem] + [vmem] * 7,
        out_specs=(vmem, vmem),
        scratch_shapes=[
            pltpu.VMEM((REQS, SEQ_BLOCKS, 16, 2 * HD), BF16),
            pltpu.VMEM((SEQ_BLOCKS, 2 * REQS, 16, 2 * HD), BF16),
            pltpu.VMEM((SEQ_BLOCKS // 2, HD, 2 * HD), BF16),
            pltpu.VMEM((SEQ_BLOCKS, HD, HD), jnp.int32),
            pltpu.VMEM((ROWS, 2 * HD), BF16),
            pltpu.VMEM((ROWS, 2 * HD), BF16),
            pltpu.VMEM((HD, HD), BF16),
            pltpu.VMEM((HD, HD), jnp.int32),
            pltpu.VMEM((SEQ_BLOCKS, 1, HD), jnp.int32),
            pltpu.VMEM((2, HD, 2 * HD), BF16),
            pltpu.VMEM((2, STEPS, 2, HD, 2 * HD), BF16),
            pltpu.VMEM((ROWS, HD), BF16),
            pltpu.VMEM((2, STEPS, ROWS, HD), BF16),
            pltpu.VMEM((18, HD, 2 * HD), F32),
            pltpu.VMEM((18, 8, 2 * HD), F32),
            pltpu.VMEM((2, STEPS, 2, HD, 2 * HD), BF16),
            pltpu.VMEM((2, STEPS, 2, 8, HD), F32),
            pltpu.VMEM((2, STEPS, 2, HD, 2 * HD), BF16),
            pltpu.VMEM((2, STEPS, 2, 8, HD), F32),
            pltpu.VMEM((8, 1, HD), F32),
            pltpu.VMEM((8, 1, HD), F32),
            pltpu.VMEM((CTX, 1, HD), F32),
            dma((2, REQS)), dma((2 * REQS,)),
            dma((SEQ_BLOCKS,)), dma((SEQ_BLOCKS,)),
            dma((1,)), dma((1,)),
            dma((2, STEPS, 2)), dma((2, STEPS, 2)),
            dma((2, STEPS)), dma((2, STEPS)),
            dma((2, STEPS, 2)), dma((2, STEPS, 2)),
            dma((2, STEPS, 2)), dma((2, STEPS, 2)),
            dma((8,)), dma((8,)),
            dma((CTX,)), dma((CTX,)),
        ],
        compiler_params=pltpu.CompilerParams(
            collective_id=0, has_side_effects=True, vmem_limit_bytes=40 * 2**20
        ),
    )(passage_lists, slot_map, rec_pos, fresh_q, fresh_kv, pool_kv, freq, cosine, sine)
    return output, deviation.reshape(ROWS)


def solution(mesh):
    in_specs = (
        P("pool", "ctx"),
        P("pool", "ctx"),
        P(None, "pool", "ctx"),
        P(),
        P(),
        P("pool", None),
    )
    out_specs = (P("pool", "ctx"), P("pool"))
    return jax.shard_map(
        on_device, mesh=mesh, in_specs=in_specs, out_specs=out_specs, check_vma=False
    )
```

profile of v0, /device:TPU:12, one launch (start us, length us, event | category | flops | bytes accessed | tf_op | source)
XLA Modules:
  0.0 110.2 jit_solution(12641552804093115543)
XLA Ops:
  0.6 0.0 copy-start
  0.6 1.2 %copy-done = bf16[256,8,256]{2,1,0:T(8,128)(2,1)S(1)} copy-done((bf16[256,8,256]{2,1,0:T(8,128)(2,1)S(1)}, bf16[256,8,256]{2,1,0:T(8,128)(2,1)}, u32[]{:S(2)}) %copy-start) | copy-done | bytes 1048600
  1.9 0.0 copy-start.1
  1.9 0.9 copy-done.1
  2.8 0.0 copy-start.2
  2.8 0.8 copy-done.2
  3.5 0.0 copy-start.3
  3.5 0.7 copy-done.3
  4.2 0.0 copy-start.4
  4.2 0.7 copy-done.4
  5.0 0.0 copy-start.5
  5.0 0.7 copy-done.5
  5.6 0.0 copy-start.6
  5.6 0.7 copy-done.6
  6.3 0.0 copy-start.7
  6.3 0.7 copy-done.7
  7.0 0.0 copy-start.8
  7.0 0.7 copy-done.8
  7.6 101.4 %shard_map.104 = (bf16[64,1024]{1,0:T(8,128)(2,1)S(1)}, f32[1,64]{1,0:T(1,128)S(1)}) custom-call(s32[4,32]{1,0:T(4,128)S(1)} %copy-done.5, s32[256]{0:T(256)S(1)} %copy-done.6, s32[1,64]{1,0:T(1,128)S(1)} %copy-done.7, bf16[64,1024]{1,0:T(8,128)(2,1)S(1)} %copy-done.1, bf16[64,256]{1,0:T(8,128)(2,1)S(1)} %copy-done.2, bf16[256,8,256]{2,1,0:T(8,128)(2,1)S(1)} %copy-done, ...), custom_call_target="tpu_custom_call" | custom-call | tf_op jit(solution)/shard_map/pallas_call | solution.py:437
  109.1 0.7 copy.13
  109.7 0.5 copy.14
Async XLA Ops:
  0.6 1.2 %copy-start = (bf16[256,8,256]{2,1,0:T(8,128)(2,1)S(1)}, bf16[256,8,256]{2,1,0:T(8,128)(2,1)}, u32[]{:S(2)}) copy-start(bf16[256,8,256]{2,1,0:T(8,128)(2,1)} %pool_ref.1) | copy-start | bytes 3145732
  1.9 0.9 copy-start.1
  2.8 0.8 copy-start.2
  3.5 0.7 copy-start.3
  4.2 0.7 copy-start.4
  5.0 0.7 copy-start.5
  5.6 0.7 copy-start.6
  6.3 0.7 copy-start.7
  7.0 0.7 copy-start.8
where the time goes:
time: 111 us; the launch traced here: 110 us
  Pallas kernels  101 us (91%)
  local copies, waits for them, and re-layouts  8.15 us (7%)
    pallas_call x1, Pallas kernels, on_device(): pl.pallas_call(kernel, out_shape=(jax.ShapeDtypeStruct((ROWS, HEADS // CT...  101 us
    unnamed x20, local copies, waits for them, and re-layouts  8.15 us

commit v1 on v0

v1 whole, which is shorter than its diff:
```python
import math

import jax
import jax.numpy as jnp
import numpy as np
from jax import lax
from jax.experimental import pallas as pl
from jax.experimental.pallas import tpu as pltpu
from jax.sharding import PartitionSpec as P

HEADS = 64
KVH = 8
HD = 128
PASSAGE = 512
BLOCK_PASSAGES = 2
SEQ_BLOCKS = 16
ROWS = 64
REQS = 4
CTX = 8
SPAN = BLOCK_PASSAGES * PASSAGE
BASE = 500000.0

MESH = pl.DeviceIdType.MESH
F32 = jnp.float32
BF16 = jnp.bfloat16
LOG2_SCALE = math.log2(math.e) / math.sqrt(HD)
NEG = -1e30
FAR = 1 << 30
WIDE = 4 * HD
PIECE = 4
GROUP = 4
STEPS = 4


def frequency_table():
    exponent = np.arange(HD // 2, dtype=np.float32) * np.float32(-2.0 * math.log(BASE) / HD)
    return np.exp(exponent.astype(np.float64)).astype(np.float32)


def angle_table():
    freq = frequency_table()
    offsets = np.arange(SEQ_BLOCKS * BLOCK_PASSAGES).astype(np.float32) * np.float32(PASSAGE)
    angles = (offsets[:, None] * freq[None, :]).astype(np.float64)
    cosine, sine = np.cos(angles), np.sin(angles)
    rows = [
        np.concatenate([cosine, cosine], axis=1),
        np.concatenate([-sine, sine], axis=1),
        np.tile(freq, 2)[None, :],
        np.zeros((7, HD)),
    ]
    return np.concatenate(rows, axis=0).astype(np.float32)


def turned(vectors, cosine, signed_sine):
    half = HD // 2
    swapped = jnp.concatenate([vectors[:, half:], vectors[:, :half]], axis=1)
    return vectors * cosine + swapped * signed_sine


def iota(shape, axis):
    return lax.broadcasted_iota(jnp.int32, shape, axis)


def kernel(
    lists_in, slots_in, rec_in, q_in, fkv_in, pool_in, table_in,
    out_ref, dev_ref,
    lists, slots, rec_ref, q_ref, fkv_ref, pool_ref, table,
    pack, kvb, vt, kpos, fkv, fkv_next, vtf, fpos, recs, qown, qbuf,
    kf_own, meta, sbuf, wbuf, part, pstat, osend, ssend, orecv, srecv, dsend, drecv, cbuf, xbuf,
    ready, ready_4, ready_8, in_s, kv_ss, kv_rs, rec_ss, rec_rs, f_ss, f_rs, q_ss, q_rs, m_ss, m_rs,
    o_ss, o_rs, s_ss, s_rs, d_ss, d_rs, c_ss, c_rs, x_ss, x_rs,
):
    where = lax.axis_index("pool")
    me_ctx = lax.axis_index("ctx")
    y = where >> 4
    z = where & (SEQ_BLOCKS - 1)

    def node(row, column):
        return {"pool": ((row & (REQS - 1)) << 4) + ((column + SEQ_BLOCKS) & (SEQ_BLOCKS - 1))}

    def remote(src, dst, send, recv, target):
        return pltpu.make_async_remote_copy(
            src_ref=src, dst_ref=dst, send_sem=send, recv_sem=recv,
            device_id=target, device_id_type=MESH,
        )

    inputs = [
        pltpu.make_async_copy(src, dst, in_s.at[i])
        for i, (src, dst) in enumerate(
            [
                (q_in, q_ref), (rec_in, rec_ref), (table_in, table), (fkv_in, fkv_ref),
                (lists_in, lists), (slots_in, slots), (pool_in, pool_ref),
            ]
        )
    ]
    for copy in inputs:
        copy.start()

    barrier = pltpu.get_barrier_semaphore()

    def greet(target):
        pl.semaphore_signal(barrier, inc=1, device_id=target, device_id_type=MESH)

    chips = CTX // 2
    core, chip = me_ctx & 1, me_ctx >> 1

    def same_core(k):
        return ((chip + k) & (chips - 1)) * 2 + core

    for k in (-2, -1, 1, 2):
        greet(node(y, z + k))
    for row in range(1, REQS):
        greet(node(y + row, z))
    greet({"ctx": me_ctx + 1 - 2 * core})
    for k in range(1, chips):
        greet({"ctx": same_core(k)})

    for copy in inputs[:4]:
        copy.wait()
    rec_row = rec_ref[...]
    rec_pair = jnp.concatenate([rec_row, rec_row], axis=1)
    recs[z] = rec_pair
    diagonal = iota((HD, HD), 0) == iota((HD, HD), 1)

    def as_column(row):
        wide = jnp.broadcast_to(row.astype(F32), (HD, HD))
        return jnp.sum(jnp.where(diagonal, wide, 0.0), axis=1, keepdims=True)

    rows_at = as_column(rec_pair)[:ROWS] + (z * SPAN).astype(F32)
    angles = rows_at * table[64:65, :]
    cosine = jnp.cos(angles)
    sine = jnp.sin(angles)
    sine = jnp.where(iota((ROWS, HD), 1) < HD // 2, -sine, sine)
    for pair in range(4):
        both = [
            turned(q_ref[:, (2 * pair + i) * HD : (2 * pair + i + 1) * HD].astype(F32), cosine, sine)
            for i in range(2)
        ]
        stacked = jnp.concatenate(both, axis=0)
        qown[pair] = stacked.T.astype(BF16)
    fresh_key = turned(fkv_ref[:, :HD].astype(F32), cosine, sine).astype(BF16)
    kf_own[...] = fresh_key
    fkv[:, :HD] = fresh_key
    fkv[:, HD:] = fkv_ref[:, HD:]
    for copy in inputs[4:]:
        copy.wait()

    def pack_for(request):
        @pl.loop(0, SEQ_BLOCKS, unroll=16)
        def _(block):
            keys, values = [], []
            for p in range(BLOCK_PASSAGES):
                passage = block * BLOCK_PASSAGES + p
                stored = pool_ref[slots[lists[request, passage]]]
                keys.append(
                    turned(
                        stored[:, :HD].astype(F32),
                        table[pl.ds(passage, 1), :],
                        table[pl.ds(passage + 32, 1), :],
                    )
                )
                values.append(stored[:, HD:].astype(F32))
            pack[request, block, :, :HD] = jnp.concatenate(keys, axis=0).astype(BF16)
            pack[request, block, :, HD:] = jnp.concatenate(values, axis=0).astype(BF16)

    for step in range(REQS):
        pack_for(step)

    pl.semaphore_wait(barrier, 4 + (REQS - 1) + 1 + chips - 1)
    for row in range(1, REQS):
        pl.semaphore_signal(ready, inc=1, device_id=node(y + row, z), device_id_type=MESH)
    for k in (-2, 2):
        pl.semaphore_signal(ready_4, inc=1, device_id=node(y, z + k), device_id_type=MESH)

    def along(d):
        return node(y, z + (2 - 4 * d))

    def q_copy(d, s, c):
        src = qown.at[c] if s == 0 else qbuf.at[d, s - 1, c]
        return remote(src, qbuf.at[d, s, c], q_ss.at[d, s, c], q_rs.at[d, s, c], along(d))

    def in_turn(first=0, count=4):
        return [((k + 2 * d) % 4, d) for k in range(first, first + count) for d in range(2)]

    def meta_copy(d, s):
        src = kf_own if s == 0 else meta.at[d, s - 1]
        return remote(src, meta.at[d, s], m_ss.at[d, s], m_rs.at[d, s], along(d))

    def side(row_a, row_b):
        return ((row_a + row_b) & 2) - 1

    def kv_copy(i, step, first=0, count=SEQ_BLOCKS):
        row = (y + step) & (REQS - 1)
        shift = side(y, row) if i else 0
        slot = i * REQS + y
        blocks = pl.ds(first, count)
        return remote(
            pack.at[row, blocks], kvb.at[blocks, slot], kv_ss.at[i, step], kv_rs.at[slot],
            node(row, z + shift),
        )

    def rec_copy(k):
        return remote(recs.at[z], recs.at[z], rec_ss.at[k], rec_rs.at[z], node(y, z + k))

    def fresh_copy():
        return remote(fkv, fkv_next, f_ss.at[0], f_rs.at[0], node(y, z + 1))

    def stat_copy(d, s, h):
        return remote(
            ssend.at[d, s, h], srecv.at[d, s, h], s_ss.at[d, s, h], s_rs.at[d, s, h], along(1 - d)
        )

    def out_copy(d, s, c):
        return remote(
            osend.at[d, s, c], orecv.at[d, s, c], o_ss.at[d, s, c], o_rs.at[d, s, c], along(1 - d)
        )

    def dev_copy(k):
        return remote(dsend.at[k], drecv.at[k], d_ss.at[k], d_rs.at[k], node(y, z - 2 * k))

    def core_copy():
        return remote(cbuf.at[0], cbuf.at[1], c_ss.at[0], c_rs.at[0], {"ctx": me_ctx + 1 - 2 * core})

    def chip_copy(k):
        return remote(
            xbuf.at[chip], xbuf.at[chip], x_ss.at[k], x_rs.at[chip], {"ctx": same_core(k)}
        )

    own_kv = pltpu.make_async_copy(pack.at[y], kvb.at[:, y], kv_rs.at[y])
    for c, d in in_turn(0, 2):
        q_copy(d, 0, c).start()
    own_kv.start()

    def kv_piece(i, n):
        for step in (2, 1, 3, 0):
            if i or step:
                kv_copy(i, step, n * PIECE, PIECE).start()

    kv_piece(0, 0)
    for c, d in in_turn(2, 1):
        q_copy(d, 0, c).start()
    pl.semaphore_wait(ready, REQS - 1)
    kv_piece(1, 0)
    for c, d in in_turn(3, 1):
        q_copy(d, 0, c).start()
    pl.semaphore_wait(ready_4, 2)
    for k in (-4, 4):
        pl.semaphore_signal(ready_8, inc=1, device_id=node(y, z + k), device_id_type=MESH)
    for i in range(2):
        kv_piece(i, 1)
    pl.semaphore_wait(ready_8, 2)
    for k in (8, 7, 9, 6, 10, 5, 11, 4, 12, 3, 13, 2, 14, 1, 15):
        rec_copy(k).start()
    for n in (2, 3):
        for i in range(2):
            kv_piece(i, n)
    for d in range(2):
        meta_copy(d, 0).start()
    fresh_copy().start()

    def q_on(d, s, c):
        q_copy(d, s, c).wait_recv()
        if s < STEPS - 2 or (s == STEPS - 2 and c // 2 == d):
            q_copy(d, s + 1, c).start()

    def meta_on(d, s):
        meta_copy(d, s).wait_recv()
        if s < STEPS - 2 or (s == STEPS - 2 and d == 0):
            meta_copy(d, s + 1).start()

    key = iota((HD, HD), 0)
    key_row = (key >> 4) & 3
    key_side = ((y + key_row) & 3) & 2
    key_column = (z - (key >> 6) * (key_side - 1) + SEQ_BLOCKS) & (SEQ_BLOCKS - 1)
    offset = ((key >> 3) & 1) * PASSAGE + key_row * 128 + key_column * 8 + (key & 7)

    def tile_of(d, s):
        return (z - (2 - 4 * d) * (s + 1) + SEQ_BLOCKS) & (SEQ_BLOCKS - 1)

    def step_on(s):
        for c, d in in_turn():
            q_on(d, s, c)
        for d in range(2):
            meta_on(d, s)

    step_on(0)
    for k in range(1, SEQ_BLOCKS):
        other = (z + k) & (SEQ_BLOCKS - 1)
        remote(
            recs.at[z], recs.at[other], rec_ss.at[k], rec_rs.at[other], node(y, z + k)
        ).wait_recv()

    @pl.loop(0, SEQ_BLOCKS, unroll=2)
    def _(block):
        same = jnp.where(offset == recs[block], 1.0, 0.0)
        replaced = jnp.max(same, axis=1, keepdims=True) > 0.0
        kpos[block] = jnp.where(replaced, FAR, offset + block * SPAN)

    before = (z + SEQ_BLOCKS - 1) & (SEQ_BLOCKS - 1)
    fresh_row = jnp.where(
        iota((1, HD), 1) < ROWS, recs[z] + z * SPAN, recs[before] + before * SPAN
    )
    fpos[...] = jnp.broadcast_to(as_column(fresh_row), (HD, HD)).astype(jnp.int32)

    step_on(1)

    for slot in range(2 * REQS):
        pltpu.make_async_copy(pack.at[0], kvb.at[:, slot], kv_rs.at[slot]).wait()
    fresh_copy().wait_recv()

    @pl.loop(0, SEQ_BLOCKS // GROUP)
    def _(g):
        for i in range(GROUP):
            values = kvb[pl.ds(GROUP * g + i, 1), :, :, HD:].reshape(HD, HD)
            vt[g, :, i * HD : (i + 1) * HD] = values.astype(F32).T.astype(BF16)

    fresh_values = jnp.concatenate([fkv[:, HD:], fkv_next[:, HD:]], axis=0)
    vtf[...] = fresh_values.astype(F32).T.astype(BF16)

    def score(query, at, blocks):
        top = None
        for i, (keys, places) in enumerate(blocks):
            seen = places <= at
            scores = jnp.dot(keys, query, preferred_element_type=F32)
            scores = jnp.where(jnp.concatenate([seen] * 4, axis=1), scores, NEG)
            sbuf[i] = scores
            largest = jnp.max(scores.reshape(HD // 8, 8, WIDE), axis=0)
            top = largest if top is None else jnp.maximum(top, largest)
        return jnp.max(top, axis=0, keepdims=True)

    def weigh(top, count):
        total = None
        for i in range(count):
            weights = jnp.exp2((sbuf[i] - top) * LOG2_SCALE)
            summed = jnp.sum(weights.reshape(HD // 8, 8, WIDE), axis=0)
            total = summed if total is None else total + summed
            wbuf[i * HD : (i + 1) * HD, :] = weights.astype(BF16)
        return jnp.sum(total, axis=0, keepdims=True)

    def stored(g):
        return [
            (kvb[g * GROUP + i, :, :, :HD].reshape(HD, HD), kpos[g * GROUP + i])
            for i in range(GROUP)
        ]

    def attend(tile, queries, job):
        at = recs[tile] + tile * SPAN
        query = jnp.concatenate([one[...] for one in queries], axis=1)
        fresh_keys = jnp.concatenate([fkv[:, :HD], fkv_next[:, :HD]], axis=0)
        top = score(query, at, [(fresh_keys, fpos[...])] + stored(0))
        total = weigh(top, GROUP + 1)
        part[job] = jnp.dot(vtf[...], wbuf[:HD, :], preferred_element_type=F32) + jnp.dot(
            vt[0], wbuf[HD:, :], preferred_element_type=F32
        )
        pstat[job, 0:1, :] = top
        pstat[job, 1:2, :] = total

        @pl.loop(1, (tile >> 2) + 1)
        def _(g):
            old_top = pstat[job, 0:1, :]
            top = jnp.maximum(old_top, score(query, at, stored(g)))
            total = weigh(top, GROUP)
            factor = jnp.exp2((old_top - top) * LOG2_SCALE)
            part[job] = part[job] * factor + jnp.dot(
                vt[g], wbuf[: GROUP * HD, :], preferred_element_type=F32
            )
            pstat[job, 0:1, :] = top
            pstat[job, 1:2, :] = pstat[job, 1:2, :] * factor + total

    def job_of(d, s):
        return 7 if s == STEPS - 1 else 1 + 2 * s + d

    def jobs(s):
        @pl.loop(0, 2)
        def _(d):
            attend(tile_of(d, s), [qbuf.at[d, s, c] for c in range(4)], 1 + 2 * s + d)

    def gap_of(tile, keys, k):
        same = jnp.where(offset == recs[tile], 1.0, 0.0)[:, :ROWS].astype(BF16)
        cached = kvb[pl.ds(tile, 1), :, :, :HD].reshape(HD, HD)
        over = (((0,), (0,)), ((), ()))
        found = lax.dot_general(same, cached, over, preferred_element_type=F32)
        hit = lax.dot_general(same, jnp.ones((HD, HD), BF16), over, preferred_element_type=F32)
        gap = (found - keys.astype(F32)) * hit
        squares = (gap * gap).T
        dsend[k, :, :ROWS] = jnp.sum(squares, axis=0, keepdims=True)

    def stats_of(job, h):
        columns = slice(h * 2 * HD, (h + 1) * 2 * HD)
        return pstat[job, 0:1, columns], pstat[job, 1:2, columns]

    def part_of(job, c):
        return part[job, :, c * HD : (c + 1) * HD]

    def combine(d, s, h, job):
        top, total = stats_of(job, h)
        stat_copy(d, s, h).wait_recv()
        other = srecv[d, s, h]
        other_top = jnp.concatenate([other[0:1, :], other[1:2, :]], axis=1)
        other_total = jnp.concatenate([other[2:3, :], other[3:4, :]], axis=1)
        new_top = jnp.maximum(top, other_top)
        mine = jnp.exp2((top - new_top) * LOG2_SCALE)
        theirs = jnp.exp2((other_top - new_top) * LOG2_SCALE)
        return new_top, total * mine + other_total * theirs, mine, theirs

    def summed(d, s, h, i, job, mine, theirs):
        columns = slice(i * HD, (i + 1) * HD)
        out_copy(d, s, 2 * h + i).wait_recv()
        far = orecv[d, s, 2 * h + i].astype(F32)
        return part_of(job, 2 * h + i) * mine[:, columns] + far * theirs[:, columns]

    def hand_on(s, furthest):
        first = s == STEPS - 1 or (s == STEPS - 2 and not furthest)
        factors = []
        for d in range(2):
            h = d if furthest else 1 - d
            job = job_of(d, s)
            if first:
                top, total = stats_of(job, h)
                factors.append(None)
            else:
                top, total, mine, theirs = combine(d, s + 1, h, job)
                factors.append((mine, theirs))
            ssend[d, s, h, 0:1, :] = top[:, :HD]
            ssend[d, s, h, 1:2, :] = top[:, HD:]
            ssend[d, s, h, 2:3, :] = total[:, :HD]
            ssend[d, s, h, 3:4, :] = total[:, HD:]
            stat_copy(d, s, h).start()
        for i in range(2):
            for d in range(2):
                h = d if furthest else 1 - d
                job = job_of(d, s)
                if first:
                    acc = part_of(job, 2 * h + i)
                else:
                    acc = summed(d, s + 1, h, i, job, *factors[d])
                osend[d, s, 2 * h + i] = acc.astype(BF16)
                out_copy(d, s, 2 * h + i).start()

    def gaps(s):
        for d in range(2 if s < STEPS - 1 else 1):
            k = s + 1 if d == 0 else SEQ_BLOCKS // 2 - s - 1
            gap_of(tile_of(d, s), meta[d, s], k)
            dev_copy(k).start()

    dsend[...] = jnp.zeros_like(dsend)
    attend(z, [qown.at[c] for c in range(4)], 0)
    jobs(0)
    step_on(2)
    jobs(1)
    jobs(2)
    for c, d in in_turn(0, 2):
        q_copy(d, 3, c).wait_recv()
    attend(tile_of(0, 3), [qbuf.at[c // 2, 3, c] for c in range(4)], 7)
    hand_on(3, True)
    hand_on(2, False)
    meta_copy(0, 3).wait_recv()
    gaps(3)
    gaps(2)
    hand_on(2, True)
    gaps(1)
    hand_on(1, False)
    gaps(0)
    gap_of(z, fkv[:, :HD], 0)
    hand_on(1, True)
    hand_on(0, False)
    for k in range(1, 8):
        dev_copy(k).wait_recv()
    shared = dsend[0]
    for k in range(1, 8):
        shared = shared + drecv[k]
    cbuf[0] = shared
    core_copy().start()
    hand_on(0, True)
    core_copy().wait_recv()
    xbuf[chip] = cbuf[0] + cbuf[1]
    for k in range(1, chips):
        chip_copy(k).start()

    def home(d, h):
        top, total, mine, theirs = combine(d, 0, h, 0)
        columns = slice(h * 2 * HD, (h + 1) * 2 * HD)
        pstat[0, 0:1, columns] = top
        pstat[0, 1:2, columns] = total
        for i in range(2):
            acc = summed(d, 0, h, i, 0, mine, theirs)
            part[0, :, (2 * h + i) * HD : (2 * h + i + 1) * HD] = acc

    for h in range(2):
        home(1 - h, h)
    for k in range(1, chips):
        other = (chip + k) & (chips - 1)
        remote(
            xbuf.at[chip], xbuf.at[other], x_ss.at[k], x_rs.at[other], {"ctx": same_core(k)}
        ).wait_recv()
    gathered = xbuf[0]
    for k in range(1, chips):
        gathered = gathered + xbuf[k]
    dev_ref[...] = gathered[:, :ROWS] / (KVH * HD)

    for h in range(2):
        home(h, h)
        for pair in range(2):
            columns = slice((2 * h + pair) * HD, (2 * h + pair + 1) * HD)
            upright = (part[0, :, columns] / pstat[0, 1:2, columns]).T.astype(BF16)
            for i in range(2):
                head = h * 4 + pair * 2 + i
                out_ref[:, head * HD : (head + 1) * HD] = upright[i * ROWS : (i + 1) * ROWS]

    for k in range(1, SEQ_BLOCKS):
        rec_copy(k).wait_send()
    for k in range(1, 8):
        dev_copy(k).wait_send()
    for step in range(REQS):
        if step:
            kv_copy(0, step).wait_send()
        kv_copy(1, step).wait_send()
    fresh_copy().wait_send()
    for d in range(2):
        for s in range(STEPS):
            for c in range(4):
                if s < STEPS - 1 or c // 2 == d:
                    q_copy(d, s, c).wait_send()
                    out_copy(d, s, c).wait_send()
                    if c % 2 == 0:
                        stat_copy(d, s, c // 2).wait_send()
            if s < STEPS - 1 or d == 0:
                meta_copy(d, s).wait_send()
    core_copy().wait_send()
    for k in range(1, chips):
        chip_copy(k).wait_send()


def on_device(fresh_q, fresh_kv, pool_kv, passage_lists, slot_map, rec_pos):
    vmem = pl.BlockSpec(memory_space=pltpu.VMEM)
    anywhere = pl.BlockSpec(memory_space=pl.ANY)
    dma = pltpu.SemaphoreType.DMA
    scratch = [
        pltpu.SMEM(passage_lists.shape, jnp.int32),
        pltpu.SMEM(slot_map.shape, jnp.int32),
        pltpu.VMEM(rec_pos.shape, jnp.int32),
        pltpu.VMEM(fresh_q.shape, BF16),
        pltpu.VMEM(fresh_kv.shape, BF16),
        pltpu.VMEM(pool_kv.shape, BF16),
        pltpu.VMEM((72, HD), F32),
        pltpu.VMEM((REQS, SEQ_BLOCKS, 16, 2 * HD), BF16),
        pltpu.VMEM((SEQ_BLOCKS, 2 * REQS, 16, 2 * HD), BF16),
        pltpu.VMEM((SEQ_BLOCKS // GROUP, HD, GROUP * HD), BF16),
        pltpu.VMEM((SEQ_BLOCKS, HD, HD), jnp.int32),
        pltpu.VMEM((ROWS, 2 * HD), BF16),
        pltpu.VMEM((ROWS, 2 * HD), BF16),
        pltpu.VMEM((HD, HD), BF16),
        pltpu.VMEM((HD, HD), jnp.int32),
        pltpu.VMEM((SEQ_BLOCKS, 1, HD), jnp.int32),
        pltpu.VMEM((4, HD, HD), BF16),
        pltpu.VMEM((2, STEPS, 4, HD, HD), BF16),
        pltpu.VMEM((ROWS, HD), BF16),
        pltpu.VMEM((2, STEPS, ROWS, HD), BF16),
        pltpu.VMEM((GROUP + 1, HD, WIDE), F32),
        pltpu.VMEM(((GROUP + 1) * HD, WIDE), BF16),
        pltpu.VMEM((8, HD, WIDE), F32),
        pltpu.VMEM((8, 8, WIDE), F32),
        pltpu.VMEM((2, STEPS, 4, HD, HD), BF16),
        pltpu.VMEM((2, STEPS, 2, 4, HD), F32),
        pltpu.VMEM((2, STEPS, 4, HD, HD), BF16),
        pltpu.VMEM((2, STEPS, 2, 4, HD), F32),
        pltpu.VMEM((8, 1, HD), F32),
        pltpu.VMEM((8, 1, HD), F32),
        pltpu.VMEM((2, 1, HD), F32),
        pltpu.VMEM((CTX // 2, 1, HD), F32),
        pltpu.SemaphoreType.REGULAR,
        pltpu.SemaphoreType.REGULAR,
        pltpu.SemaphoreType.REGULAR,
        dma((7,)),
        dma((2, REQS)), dma((2 * REQS,)),
        dma((SEQ_BLOCKS,)), dma((SEQ_BLOCKS,)),
        dma((1,)), dma((1,)),
        dma((2, STEPS, 4)), dma((2, STEPS, 4)),
        dma((2, STEPS)), dma((2, STEPS)),
        dma((2, STEPS, 4)), dma((2, STEPS, 4)),
        dma((2, STEPS, 2)), dma((2, STEPS, 2)),
        dma((8,)), dma((8,)),
        dma((1,)), dma((1,)),
        dma((CTX // 2,)), dma((CTX // 2,)),
    ]
    output, deviation = pl.pallas_call(
        kernel,
        out_shape=(
            jax.ShapeDtypeStruct((ROWS, HEADS // CTX * HD), BF16),
            jax.ShapeDtypeStruct((1, ROWS), F32),
        ),
        in_specs=[anywhere] * 7,
        out_specs=(vmem, vmem),
        scratch_shapes=scratch,
        compiler_params=pltpu.CompilerParams(
            collective_id=0, has_side_effects=True, vmem_limit_bytes=60 * 2**20
        ),
    )(passage_lists, slot_map, rec_pos, fresh_q, fresh_kv, pool_kv, jnp.asarray(angle_table()))
    return output, deviation.reshape(ROWS)


def solution(mesh):
    in_specs = (
        P("pool", "ctx"),
        P("pool", "ctx"),
        P(None, "pool", "ctx"),
        P(),
        P(),
        P("pool", None),
    )
    out_specs = (P("pool", "ctx"), P("pool"))
    return jax.shard_map(
        on_device, mesh=mesh, in_specs=in_specs, out_specs=out_specs, check_vma=False
    )
```

time: 111 us -> 80.3 us (0.72)
  the two profiles are of different devices: /device:TPU:12 before, /device:TPU:1 now
where the time goes in v1:
time: 80.3 us; the launch traced here: 80.1 us
  Pallas kernels  77.4 us (96%)
  local copies, waits for them, and re-layouts  2.08 us (3%)
    pallas_call x1, Pallas kernels, on_device(): pl.pallas_call(kernel, out_shape=(jax.ShapeDtypeStruct((ROWS, HEADS // CT...  77.4 us
    unnamed x4, local copies, waits for them, and re-layouts  2.08 us

profile of v1, /device:TPU:1, one launch (start us, length us, event | category | flops | bytes accessed | tf_op | source)
XLA Modules:
  0.0 80.1 jit_solution(5222731407433976387)
XLA Ops:
  0.6 77.4 %shard_map.86 = (bf16[64,1024]{1,0:T(8,128)(2,1)}, f32[1,64]{1,0:T(1,128)}) custom-call(s32[4,32]{1,0:T(4,128)} %lists_in.1, s32[256]{0:T(256)} %slots_in.1, s32[1,64]{1,0:T(1,128)} %rec_in.1, bf16[64,1024]{1,0:T(8,128)(2,1)} %q_in.1, bf16[64,256]{1,0:T(8,128)(2,1)} %fkv_in.1, bf16[256,8,256]{2,1,0:T(8,128)(2,1)} %pool_in.1, f32[72,128]{1,0:T(8,128)} %constant.2.clone.table_in), custom_call_target="tpu_custom_call" | custom-call | tf_op jit(solution)/shard_map/pallas_call | solution.py:586
  78.0 0.0 copy-start
  78.0 1.6 %copy.11 = bf16[64,1024]{1,0:T(8,128)(2,1)} copy(bf16[64,1024]{1,0:T(8,128)(2,1)} %get-tuple-element.8) | data formatting | bytes 262144
  79.6 0.0 copy-done
  79.6 0.5 copy.12
Async XLA Ops:
  78.0 1.6 %copy-start = (f32[1,64]{1,0:T(1,128)S(1)}, f32[1,64]{1,0:T(1,128)}, u32[]{:S(2)}) copy-start(f32[1,64]{1,0:T(1,128)} %get-tuple-element.5) | copy-start | bytes 772

commit v2 on v1

--- a/solution.py
+++ b/solution.py
@@ -66,7 +66,7 @@
     out_ref, dev_ref,
     lists, slots, rec_ref, q_ref, fkv_ref, pool_ref, table,
     pack, kvb, vt, kpos, fkv, fkv_next, vtf, fpos, recs, qown, qbuf,
-    kf_own, meta, sbuf, wbuf, part, pstat, osend, ssend, orecv, srecv, dsend, drecv, cbuf, xbuf,
+    kf_own, meta, sbuf, part, pstat, osend, ssend, orecv, srecv, dsend, drecv, cbuf, xbuf,
     ready, ready_4, ready_8, in_s, kv_ss, kv_rs, rec_ss, rec_rs, f_ss, f_rs, q_ss, q_rs, m_ss, m_rs,
     o_ss, o_rs, s_ss, s_rs, d_ss, d_rs, c_ss, c_rs, x_ss, x_rs,
 ):
@@ -119,7 +119,7 @@
         copy.wait()
     rec_row = rec_ref[...]
     rec_pair = jnp.concatenate([rec_row, rec_row], axis=1)
-    recs[z] = rec_pair
+    recs[z, 0] = rec_pair
     diagonal = iota((HD, HD), 0) == iota((HD, HD), 1)
 
     def as_column(row):
@@ -199,8 +199,23 @@
             node(row, z + shift),
         )
 
+    def next_copy():
+        return remote(
+            recs.at[z, 0], recs.at[(z - 1) & (SEQ_BLOCKS - 1), 1], rec_ss.at[0], rec_rs.at[SEQ_BLOCKS],
+            node(y, z - 1),
+        )
+
+    def next_wait():
+        remote(
+            recs.at[z, 0], recs.at[z, 1], rec_ss.at[0], rec_rs.at[SEQ_BLOCKS], node(y, z - 1)
+        ).wait_recv()
+
     def rec_copy(k):
-        return remote(recs.at[z], recs.at[z], rec_ss.at[k], rec_rs.at[z], node(y, z + k))
+        return remote(recs.at[z], recs.at[z], rec_ss.at[k], rec_rs.at[z], node(y, z + 2 * k))
+
+    def positions(tile):
+        odd = (tile ^ z) & 1
+        return recs[(tile - odd) & (SEQ_BLOCKS - 1), odd]
 
     def fresh_copy():
         return remote(fkv, fkv_next, f_ss.at[0], f_rs.at[0], node(y, z + 1))
@@ -226,7 +241,18 @@
             xbuf.at[chip], xbuf.at[chip], x_ss.at[k], x_rs.at[chip], {"ctx": same_core(k)}
         )
 
+    def q_on(d, s, c):
+        q_copy(d, s, c).wait_recv()
+        if s < STEPS - 2 or (s == STEPS - 2 and c // 2 == d):
+            q_copy(d, s + 1, c).start()
+
+    def meta_on(d, s):
+        meta_copy(d, s).wait_recv()
+        if s < STEPS - 2 or (s == STEPS - 2 and d == 0):
+            meta_copy(d, s + 1).start()
+
     own_kv = pltpu.make_async_copy(pack.at[y], kvb.at[:, y], kv_rs.at[y])
+    next_copy().start()
     for c, d in in_turn(0, 2):
         q_copy(d, 0, c).start()
     own_kv.start()
@@ -248,25 +274,23 @@
         pl.semaphore_signal(ready_8, inc=1, device_id=node(y, z + k), device_id_type=MESH)
     for i in range(2):
         kv_piece(i, 1)
-    pl.semaphore_wait(ready_8, 2)
-    for k in (8, 7, 9, 6, 10, 5, 11, 4, 12, 3, 13, 2, 14, 1, 15):
-        rec_copy(k).start()
-    for n in (2, 3):
-        for i in range(2):
-            kv_piece(i, n)
     for d in range(2):
         meta_copy(d, 0).start()
     fresh_copy().start()
-
-    def q_on(d, s, c):
-        q_copy(d, s, c).wait_recv()
-        if s < STEPS - 2 or (s == STEPS - 2 and c // 2 == d):
-            q_copy(d, s + 1, c).start()
-
-    def meta_on(d, s):
-        meta_copy(d, s).wait_recv()
-        if s < STEPS - 2 or (s == STEPS - 2 and d == 0):
-            meta_copy(d, s + 1).start()
+    for c, d in in_turn(0, 2):
+        q_on(d, 0, c)
+    pl.semaphore_wait(ready_8, 2)
+    next_wait()
+    for k in (4, 3, 5, 2, 6, 1, 7):
+        rec_copy(k).start()
+    for i in range(2):
+        kv_piece(i, 2)
+    for c, d in in_turn(2, 2):
+        q_on(d, 0, c)
+    for i in range(2):
+        kv_piece(i, 3)
+    for d in range(2):
+        meta_on(d, 0)
 
     key = iota((HD, HD), 0)
     key_row = (key >> 4) & 3
@@ -277,32 +301,36 @@
     def tile_of(d, s):
         return (z - (2 - 4 * d) * (s + 1) + SEQ_BLOCKS) & (SEQ_BLOCKS - 1)
 
-    def step_on(s):
-        for c, d in in_turn():
+    def far_on(s):
+        for c, d in in_turn(0, 2):
+            q_on(d, s, c)
+
+    def near_on(s):
+        for c, d in in_turn(2, 2):
             q_on(d, s, c)
         for d in range(2):
             meta_on(d, s)
 
-    step_on(0)
-    for k in range(1, SEQ_BLOCKS):
-        other = (z + k) & (SEQ_BLOCKS - 1)
+    far_on(1)
+    for k in range(1, 8):
+        other = (z + 2 * k) & (SEQ_BLOCKS - 1)
         remote(
-            recs.at[z], recs.at[other], rec_ss.at[k], rec_rs.at[other], node(y, z + k)
+            recs.at[z], recs.at[other], rec_ss.at[k], rec_rs.at[other], node(y, z + 2 * k)
         ).wait_recv()
 
     @pl.loop(0, SEQ_BLOCKS, unroll=2)
     def _(block):
-        same = jnp.where(offset == recs[block], 1.0, 0.0)
+        same = jnp.where(offset == positions(block), 1.0, 0.0)
         replaced = jnp.max(same, axis=1, keepdims=True) > 0.0
         kpos[block] = jnp.where(replaced, FAR, offset + block * SPAN)
 
     before = (z + SEQ_BLOCKS - 1) & (SEQ_BLOCKS - 1)
     fresh_row = jnp.where(
-        iota((1, HD), 1) < ROWS, recs[z] + z * SPAN, recs[before] + before * SPAN
+        iota((1, HD), 1) < ROWS, positions(z) + z * SPAN, positions(before) + before * SPAN
     )
     fpos[...] = jnp.broadcast_to(as_column(fresh_row), (HD, HD)).astype(jnp.int32)
 
-    step_on(1)
+    near_on(1)
 
     for slot in range(2 * REQS):
         pltpu.make_async_copy(pack.at[0], kvb.at[:, slot], kv_rs.at[slot]).wait()
@@ -317,25 +345,33 @@
     fresh_values = jnp.concatenate([fkv[:, HD:], fkv_next[:, HD:]], axis=0)
     vtf[...] = fresh_values.astype(F32).T.astype(BF16)
 
-    def score(query, at, blocks):
+    halves = [slice(0, 2 * HD), slice(2 * HD, 4 * HD)]
+
+    def score(query, at, blocks, columns):
         top = None
         for i, (keys, places) in enumerate(blocks):
             seen = places <= at
-            scores = jnp.dot(keys, query, preferred_element_type=F32)
-            scores = jnp.where(jnp.concatenate([seen] * 4, axis=1), scores, NEG)
-            sbuf[i] = scores
-            largest = jnp.max(scores.reshape(HD // 8, 8, WIDE), axis=0)
+            scores = jnp.dot(keys, query[:, columns], preferred_element_type=F32)
+            scores = jnp.where(jnp.concatenate([seen, seen], axis=1), scores, NEG)
+            sbuf[i, :, columns] = scores
+            largest = jnp.max(scores.reshape(HD // 8, 8, 2 * HD), axis=0)
             top = largest if top is None else jnp.maximum(top, largest)
         return jnp.max(top, axis=0, keepdims=True)
 
-    def weigh(top, count):
-        total = None
-        for i in range(count):
-            weights = jnp.exp2((sbuf[i] - top) * LOG2_SCALE)
-            summed = jnp.sum(weights.reshape(HD // 8, 8, WIDE), axis=0)
-            total = summed if total is None else total + summed
-            wbuf[i * HD : (i + 1) * HD, :] = weights.astype(BF16)
-        return jnp.sum(total, axis=0, keepdims=True)
+    def weigh(top, groups, columns):
+        total, acc = None, None
+        for members, values_t in groups:
+            rounded = []
+            for i in members:
+                weights = jnp.exp2((sbuf[i, :, columns] - top) * LOG2_SCALE)
+                summed = jnp.sum(weights.reshape(HD // 8, 8, 2 * HD), axis=0)
+                total = summed if total is None else total + summed
+                rounded.append(weights.astype(BF16))
+            product = jnp.dot(
+                values_t, jnp.concatenate(rounded, axis=0), preferred_element_type=F32
+            )
+            acc = product if acc is None else acc + product
+        return jnp.sum(total, axis=0, keepdims=True), acc
 
     def stored(g):
         return [
@@ -344,28 +380,30 @@
         ]
 
     def attend(tile, queries, job):
-        at = recs[tile] + tile * SPAN
+        at = positions(tile) + tile * SPAN
         query = jnp.concatenate([one[...] for one in queries], axis=1)
         fresh_keys = jnp.concatenate([fkv[:, :HD], fkv_next[:, :HD]], axis=0)
-        top = score(query, at, [(fresh_keys, fpos[...])] + stored(0))
-        total = weigh(top, GROUP + 1)
-        part[job] = jnp.dot(vtf[...], wbuf[:HD, :], preferred_element_type=F32) + jnp.dot(
-            vt[0], wbuf[HD:, :], preferred_element_type=F32
-        )
-        pstat[job, 0:1, :] = top
-        pstat[job, 1:2, :] = total
+        blocks = [(fresh_keys, fpos[...])] + stored(0)
+        groups = [([0], vtf[...]), (list(range(1, GROUP + 1)), vt[0])]
+        tops = [score(query, at, blocks, columns) for columns in halves]
+        for columns, top in zip(halves, tops):
+            total, acc = weigh(top, groups, columns)
+            part[job, :, columns] = acc
+            pstat[job, 0:1, columns] = top
+            pstat[job, 1:2, columns] = total
 
         @pl.loop(1, (tile >> 2) + 1)
         def _(g):
-            old_top = pstat[job, 0:1, :]
-            top = jnp.maximum(old_top, score(query, at, stored(g)))
-            total = weigh(top, GROUP)
-            factor = jnp.exp2((old_top - top) * LOG2_SCALE)
-            part[job] = part[job] * factor + jnp.dot(
-                vt[g], wbuf[: GROUP * HD, :], preferred_element_type=F32
-            )
-            pstat[job, 0:1, :] = top
-            pstat[job, 1:2, :] = pstat[job, 1:2, :] * factor + total
+            groups = [(list(range(GROUP)), vt[g])]
+            tops = [score(query, at, stored(g), columns) for columns in halves]
+            for columns, top in zip(halves, tops):
+                old_top = pstat[job, 0:1, columns]
+                top = jnp.maximum(old_top, top)
+                total, acc = weigh(top, groups, columns)
+                factor = jnp.exp2((old_top - top) * LOG2_SCALE)
+                part[job, :, columns] = part[job, :, columns] * factor + acc
+                pstat[job, 0:1, columns] = top
+                pstat[job, 1:2, columns] = pstat[job, 1:2, columns] * factor + total
 
     def job_of(d, s):
         return 7 if s == STEPS - 1 else 1 + 2 * s + d
@@ -376,7 +414,7 @@
             attend(tile_of(d, s), [qbuf.at[d, s, c] for c in range(4)], 1 + 2 * s + d)
 
     def gap_of(tile, keys, k):
-        same = jnp.where(offset == recs[tile], 1.0, 0.0)[:, :ROWS].astype(BF16)
+        same = jnp.where(offset == positions(tile), 1.0, 0.0)[:, :ROWS].astype(BF16)
         cached = kvb[pl.ds(tile, 1), :, :, :HD].reshape(HD, HD)
         over = (((0,), (0,)), ((), ()))
         found = lax.dot_general(same, cached, over, preferred_element_type=F32)
@@ -444,26 +482,27 @@
             dev_copy(k).start()
 
     dsend[...] = jnp.zeros_like(dsend)
+    far_on(2)
     attend(z, [qown.at[c] for c in range(4)], 0)
-    jobs(0)
-    step_on(2)
-    jobs(1)
+    near_on(2)
     jobs(2)
+    hand_on(2, False)
     for c, d in in_turn(0, 2):
         q_copy(d, 3, c).wait_recv()
     attend(tile_of(0, 3), [qbuf.at[c // 2, 3, c] for c in range(4)], 7)
     hand_on(3, True)
-    hand_on(2, False)
+    jobs(1)
+    hand_on(1, False)
     meta_copy(0, 3).wait_recv()
     gaps(3)
     gaps(2)
     hand_on(2, True)
+    jobs(0)
+    hand_on(0, False)
     gaps(1)
-    hand_on(1, False)
     gaps(0)
     gap_of(z, fkv[:, :HD], 0)
     hand_on(1, True)
-    hand_on(0, False)
     for k in range(1, 8):
         dev_copy(k).wait_recv()
     shared = dsend[0]
@@ -507,9 +546,9 @@
                 head = h * 4 + pair * 2 + i
                 out_ref[:, head * HD : (head + 1) * HD] = upright[i * ROWS : (i + 1) * ROWS]
 
-    for k in range(1, SEQ_BLOCKS):
+    next_copy().wait_send()
+    for k in range(1, 8):
         rec_copy(k).wait_send()
-    for k in range(1, 8):
         dev_copy(k).wait_send()
     for step in range(REQS):
         if step:
@@ -551,13 +590,12 @@
         pltpu.VMEM((ROWS, 2 * HD), BF16),
         pltpu.VMEM((HD, HD), BF16),
         pltpu.VMEM((HD, HD), jnp.int32),
-        pltpu.VMEM((SEQ_BLOCKS, 1, HD), jnp.int32),
+        pltpu.VMEM((SEQ_BLOCKS, 2, 1, HD), jnp.int32),
         pltpu.VMEM((4, HD, HD), BF16),
         pltpu.VMEM((2, STEPS, 4, HD, HD), BF16),
         pltpu.VMEM((ROWS, HD), BF16),
         pltpu.VMEM((2, STEPS, ROWS, HD), BF16),
         pltpu.VMEM((GROUP + 1, HD, WIDE), F32),
-        pltpu.VMEM(((GROUP + 1) * HD, WIDE), BF16),
         pltpu.VMEM((8, HD, WIDE), F32),
         pltpu.VMEM((8, 8, WIDE), F32),
         pltpu.VMEM((2, STEPS, 4, HD, HD), BF16),
@@ -573,7 +611,7 @@
         pltpu.SemaphoreType.REGULAR,
         dma((7,)),
         dma((2, REQS)), dma((2 * REQS,)),
-        dma((SEQ_BLOCKS,)), dma((SEQ_BLOCKS,)),
+        dma((SEQ_BLOCKS,)), dma((SEQ_BLOCKS + 1,)),
         dma((1,)), dma((1,)),
         dma((2, STEPS, 4)), dma((2, STEPS, 4)),
         dma((2, STEPS)), dma((2, STEPS)),

time: 80.3 us -> 75.2 us (0.936)
  Pallas kernels: 77.4 us -> 71.6 us
    pallas_call x1, Pallas kernels: 77.4 us -> 71.6 us  [on_device(): pl.pallas_call(kernel, out_shape=(jax.ShapeDtypeStruct((ROWS, HEADS // CT...]
where the time goes in v2:
time: 75.2 us; the launch traced here: 74.4 us
  Pallas kernels  71.6 us (95%)
  local copies, waits for them, and re-layouts  2.08 us (3%)
    pallas_call x1, Pallas kernels, on_device(): pl.pallas_call(kernel, out_shape=(jax.ShapeDtypeStruct((ROWS, HEADS // CT...  71.6 us
    unnamed x4, local copies, waits for them, and re-layouts  2.08 us

profile of v2, /device:TPU:1, one launch (start us, length us, event | category | flops | bytes accessed | tf_op | source)
XLA Modules:
  0.0 74.4 jit_solution(24549456501402687)
XLA Ops:
  0.6 71.6 %shard_map.86 = (bf16[64,1024]{1,0:T(8,128)(2,1)}, f32[1,64]{1,0:T(1,128)}) custom-call(s32[4,32]{1,0:T(4,128)} %lists_in.1, s32[256]{0:T(256)} %slots_in.1, s32[1,64]{1,0:T(1,128)} %rec_in.1, bf16[64,1024]{1,0:T(8,128)(2,1)} %q_in.1, bf16[64,256]{1,0:T(8,128)(2,1)} %fkv_in.1, bf16[256,8,256]{2,1,0:T(8,128)(2,1)} %pool_in.1, f32[72,128]{1,0:T(8,128)} %constant.2.clone.table_in), custom_call_target="tpu_custom_call" | custom-call | tf_op jit(solution)/shard_map/pallas_call | solution.py:624
  72.3 0.0 copy-start
  72.3 1.6 %copy.11 = bf16[64,1024]{1,0:T(8,128)(2,1)} copy(bf16[64,1024]{1,0:T(8,128)(2,1)} %get-tuple-element.8) | data formatting | bytes 262144
  73.9 0.0 copy-done
  73.9 0.5 copy.12
Async XLA Ops:
  72.3 1.6 %copy-start = (f32[1,64]{1,0:T(1,128)S(1)}, f32[1,64]{1,0:T(1,128)}, u32[]{:S(2)}) copy-start(f32[1,64]{1,0:T(1,128)} %get-tuple-element.5) | copy-start | bytes 772

commit v3 on v2

--- a/solution.py
+++ b/solution.py
@@ -66,8 +66,8 @@
     out_ref, dev_ref,
     lists, slots, rec_ref, q_ref, fkv_ref, pool_ref, table,
     pack, kvb, vt, kpos, fkv, fkv_next, vtf, fpos, recs, qown, qbuf,
-    kf_own, meta, sbuf, part, pstat, osend, ssend, orecv, srecv, dsend, drecv, cbuf, xbuf,
-    ready, ready_4, ready_8, in_s, kv_ss, kv_rs, rec_ss, rec_rs, f_ss, f_rs, q_ss, q_rs, m_ss, m_rs,
+    out_buf, kf_own, meta, sbuf, part, pstat, osend, ssend, orecv, srecv, dsend, drecv, cbuf, xbuf,
+    ready, ready_4, ready_8, out_s, in_s, kv_ss, kv_rs, rec_ss, rec_rs, f_ss, f_rs, q_ss, q_rs, m_ss, m_rs,
     o_ss, o_rs, s_ss, s_rs, d_ss, d_rs, c_ss, c_rs, x_ss, x_rs,
 ):
     where = lax.axis_index("pool")
@@ -510,46 +510,22 @@
         shared = shared + drecv[k]
     cbuf[0] = shared
     core_copy().start()
-    hand_on(0, True)
-    core_copy().wait_recv()
-    xbuf[chip] = cbuf[0] + cbuf[1]
-    for k in range(1, chips):
-        chip_copy(k).start()
-
-    def home(d, h):
-        top, total, mine, theirs = combine(d, 0, h, 0)
-        columns = slice(h * 2 * HD, (h + 1) * 2 * HD)
-        pstat[0, 0:1, columns] = top
-        pstat[0, 1:2, columns] = total
-        for i in range(2):
-            acc = summed(d, 0, h, i, 0, mine, theirs)
-            part[0, :, (2 * h + i) * HD : (2 * h + i + 1) * HD] = acc
-
-    for h in range(2):
-        home(1 - h, h)
-    for k in range(1, chips):
-        other = (chip + k) & (chips - 1)
-        remote(
-            xbuf.at[chip], xbuf.at[other], x_ss.at[k], x_rs.at[other], {"ctx": same_core(k)}
-        ).wait_recv()
-    gathered = xbuf[0]
-    for k in range(1, chips):
-        gathered = gathered + xbuf[k]
-    dev_ref[...] = gathered[:, :ROWS] / (KVH * HD)
-
-    for h in range(2):
-        home(h, h)
-        for pair in range(2):
-            columns = slice((2 * h + pair) * HD, (2 * h + pair + 1) * HD)
-            upright = (part[0, :, columns] / pstat[0, 1:2, columns]).T.astype(BF16)
-            for i in range(2):
-                head = h * 4 + pair * 2 + i
-                out_ref[:, head * HD : (head + 1) * HD] = upright[i * ROWS : (i + 1) * ROWS]
+
+    def outs_left(s):
+        for d in range(2):
+            for c in range(4):
+                if s < STEPS - 1 or c // 2 == d:
+                    out_copy(d, s, c).wait_send()
+                    if c % 2 == 0:
+                        stat_copy(d, s, c // 2).wait_send()
+
+    def half_out(h):
+        columns = pl.ds(h * WIDE, WIDE)
+        return pltpu.make_async_copy(out_buf.at[:, columns], out_ref.at[:, columns], out_s.at[h])
 
     next_copy().wait_send()
     for k in range(1, 8):
         rec_copy(k).wait_send()
-        dev_copy(k).wait_send()
     for step in range(REQS):
         if step:
             kv_copy(0, step).wait_send()
@@ -560,14 +536,56 @@
             for c in range(4):
                 if s < STEPS - 1 or c // 2 == d:
                     q_copy(d, s, c).wait_send()
-                    out_copy(d, s, c).wait_send()
-                    if c % 2 == 0:
-                        stat_copy(d, s, c // 2).wait_send()
             if s < STEPS - 1 or d == 0:
                 meta_copy(d, s).wait_send()
+    for s in (3, 2):
+        outs_left(s)
+    hand_on(0, True)
+    core_copy().wait_recv()
+    xbuf[chip] = cbuf[0] + cbuf[1]
+    for k in range(1, chips):
+        chip_copy(k).start()
+
+    def home(d, h):
+        top, total, mine, theirs = combine(d, 0, h, 0)
+        columns = slice(h * 2 * HD, (h + 1) * 2 * HD)
+        pstat[0, 0:1, columns] = top
+        pstat[0, 1:2, columns] = total
+        for i in range(2):
+            acc = summed(d, 0, h, i, 0, mine, theirs)
+            part[0, :, (2 * h + i) * HD : (2 * h + i + 1) * HD] = acc
+
+    for h in range(2):
+        home(1 - h, h)
+    outs_left(1)
+    for k in range(1, chips):
+        other = (chip + k) & (chips - 1)
+        remote(
+            xbuf.at[chip], xbuf.at[other], x_ss.at[k], x_rs.at[other], {"ctx": same_core(k)}
+        ).wait_recv()
+    gathered = xbuf[0]
+    for k in range(1, chips):
+        gathered = gathered + xbuf[k]
+    dev_ref[...] = gathered[0, :ROWS] / (KVH * HD)
+
+    for h in range(2):
+        home(h, h)
+        for pair in range(2):
+            columns = slice((2 * h + pair) * HD, (2 * h + pair + 1) * HD)
+            upright = (part[0, :, columns] / pstat[0, 1:2, columns]).T.astype(BF16)
+            for i in range(2):
+                head = h * 4 + pair * 2 + i
+                out_buf[:, head * HD : (head + 1) * HD] = upright[i * ROWS : (i + 1) * ROWS]
+        half_out(h).start()
+
+    outs_left(0)
+    for k in range(1, 8):
+        dev_copy(k).wait_send()
     core_copy().wait_send()
     for k in range(1, chips):
         chip_copy(k).wait_send()
+    for h in range(2):
+        half_out(h).wait()
 
 
 def on_device(fresh_q, fresh_kv, pool_kv, passage_lists, slot_map, rec_pos):
@@ -593,6 +611,7 @@
         pltpu.VMEM((SEQ_BLOCKS, 2, 1, HD), jnp.int32),
         pltpu.VMEM((4, HD, HD), BF16),
         pltpu.VMEM((2, STEPS, 4, HD, HD), BF16),
+        pltpu.VMEM((ROWS, HEADS // KVH * HD), BF16),
         pltpu.VMEM((ROWS, HD), BF16),
         pltpu.VMEM((2, STEPS, ROWS, HD), BF16),
         pltpu.VMEM((GROUP + 1, HD, WIDE), F32),
@@ -609,6 +628,7 @@
         pltpu.SemaphoreType.REGULAR,
         pltpu.SemaphoreType.REGULAR,
         pltpu.SemaphoreType.REGULAR,
+        dma((2,)),
         dma((7,)),
         dma((2, REQS)), dma((2 * REQS,)),
         dma((SEQ_BLOCKS,)), dma((SEQ_BLOCKS + 1,)),
@@ -625,16 +645,16 @@
         kernel,
         out_shape=(
             jax.ShapeDtypeStruct((ROWS, HEADS // CTX * HD), BF16),
-            jax.ShapeDtypeStruct((1, ROWS), F32),
+            jax.ShapeDtypeStruct((ROWS,), F32),
         ),
         in_specs=[anywhere] * 7,
-        out_specs=(vmem, vmem),
+        out_specs=(anywhere, vmem),
         scratch_shapes=scratch,
         compiler_params=pltpu.CompilerParams(
             collective_id=0, has_side_effects=True, vmem_limit_bytes=60 * 2**20
         ),
     )(passage_lists, slot_map, rec_pos, fresh_q, fresh_kv, pool_kv, jnp.asarray(angle_table()))
-    return output, deviation.reshape(ROWS)
+    return output, deviation
 
 
 def solution(mesh):

time: 75.2 us -> 75.7 us (level)
  no operation moved by 1% of the time
where the time goes in v3:
time: 75.7 us; the launch traced here: 74.8 us
  Pallas kernels  72 us (95%)
  local copies, waits for them, and re-layouts  2.08 us (3%)
    pallas_call x1, Pallas kernels, on_device(): pl.pallas_call(kernel, out_shape=(jax.ShapeDtypeStruct((ROWS, HEADS // CT...  72 us
    unnamed x4, local copies, waits for them, and re-layouts  2.08 us

profile of v3, /device:TPU:1, one launch (start us, length us, event | category | flops | bytes accessed | tf_op | source)
XLA Modules:
  0.0 74.8 jit_solution(15686941466384915575)
XLA Ops:
  0.6 72.0 %shard_map.86 = (bf16[64,1024]{1,0:T(8,128)(2,1)}, f32[64]{0:T(128)}) custom-call(s32[4,32]{1,0:T(4,128)} %lists_in.1, s32[256]{0:T(256)} %slots_in.1, s32[1,64]{1,0:T(1,128)} %rec_in.1, bf16[64,1024]{1,0:T(8,128)(2,1)} %q_in.1, bf16[64,256]{1,0:T(8,128)(2,1)} %fkv_in.1, bf16[256,8,256]{2,1,0:T(8,128)(2,1)} %pool_in.1, f32[72,128]{1,0:T(8,128)} %constant.2.clone.table_in), custom_call_target="tpu_custom_call" | custom-call | tf_op jit(solution)/shard_map/pallas_call | solution.py:644
  72.7 0.0 copy-start
  72.7 1.6 %copy.11 = bf16[64,1024]{1,0:T(8,128)(2,1)} copy(bf16[64,1024]{1,0:T(8,128)(2,1)} %get-tuple-element.4) | data formatting | bytes 262144
  74.3 0.0 copy-done
  74.3 0.5 copy.12
Async XLA Ops:
  72.7 1.6 %copy-start = (f32[64]{0:T(128)S(1)}, f32[64]{0:T(128)}, u32[]{:S(2)}) copy-start(f32[64]{0:T(128)} %get-tuple-element.5) | copy-start | bytes 772
